TPU v7x, 32 devices: a whole 2x2x4 slice. The times are simulated.
32 devices in a mesh: dp: 4 (over y, core), tensor: 8 (over z, x).
Axes of the slice: x: 2, y: 2, z: 4, core: 2. Of those that a mesh axis runs over, the one named last changes fastest.
Arguments:
- tokens: bfloat16 [4096, 2048], P(('dp', 'tensor')), may hold values from -6 to 6
- lengths: int32 [4, 6], P('dp'), may hold values from 1 to 8, 16 in all within a row
- gain_attn: float32 [2048], replicated, may hold values from 0.25 to 1.75
- w_query: bfloat16 [2048, 2048], P(None, 'tensor'), may hold values from -0.125 to 0.125
- w_kv: bfloat16 [2048, 256], replicated, may hold values from -0.125 to 0.125
- w_attn_out: bfloat16 [2048, 2048], P('tensor'), may hold values from -1 to 1
- gain_mlp: float32 [2048], replicated, may hold values from 0.25 to 1.75
- w_gate: bfloat16 [2048, 5632], P(None, 'tensor'), may hold values from -0.125 to 0.125
- w_up: bfloat16 [2048, 5632], P(None, 'tensor'), may hold values from -0.125 to 0.125
- w_down: bfloat16 [5632, 2048], P('tensor'), may hold values from -0.078125 to 0.078125
- out_grad: bfloat16 [4096, 2048], P(('dp', 'tensor')), may hold values from -6 to 6
- kv_grad: bfloat16 [4096, 256], P(('dp', 'tensor')), may hold values from -6 to 6
Outputs:
- block_out: bfloat16 [4096, 2048], P(('dp', 'tensor'))
- grad_tokens: bfloat16 [4096, 2048], P(('dp', 'tensor'))
- grad_gain_attn: float32 [2048], P(('dp', 'tensor'))
- grad_w_query: float32 [2048, 2048], P('dp', 'tensor')
- grad_w_kv: float32 [2048, 256], P(('dp', 'tensor'))
- grad_w_attn_out: float32 [2048, 2048], P('tensor', 'dp')
- grad_gain_mlp: float32 [2048], P(('dp', 'tensor'))
- grad_w_gate: float32 [2048, 5632], P('dp', 'tensor')
- grad_w_up: float32 [2048, 5632], P('dp', 'tensor')
- grad_w_down: float32 [5632, 2048], P('tensor', 'dp')
Inputs may be any that keep to these rules, and one draw needn't show every extreme that they name: Each row of lengths gives the lengths, in units of 64 tokens, of its group's 6 pieces in order; they sum to 16, the largest is exactly 8, and the last piece is padding.
All inputs are finite; a program needn't handle non-finite values.
Results may differ from a plain program's by a relative error of at most 0.024.
Values may be sent and summed in bfloat16 or wider, within the bound.
A program may use at most 128 MiB of HBM per device.

v0:
```python
import jax
import jax.numpy as jnp
from jax import lax
from jax.sharding import PartitionSpec as P

SPAN = 64


EPSILON = 1e-05
ROTARY_BASE = 10000.0
MASKED = -1e30


def rotary_tables(positions, width):
    half_width = width // 2
    freqs = ROTARY_BASE ** (-jnp.arange(half_width, dtype=jnp.float32) / half_width)
    angles = positions[:, None] * freqs[None, :]
    return (jnp.cos(angles), jnp.sin(angles))


def rotate(values, cosine, sine):
    half_width = values.shape[-1] // 2
    first_half = values[..., :half_width]
    second_half = values[..., half_width:]
    return jnp.concatenate(
        [first_half * cosine - second_half * sine, second_half * cosine + first_half * sine],
        axis=-1,
    )


def unrotate(values, cosine, sine):
    half_width = values.shape[-1] // 2
    first_half = values[..., :half_width]
    second_half = values[..., half_width:]
    return jnp.concatenate(
        [first_half * cosine + second_half * sine, second_half * cosine - first_half * sine],
        axis=-1,
    )


def layout(piece_units, rows):
    piece_rows = piece_units * SPAN
    ends = jnp.cumsum(piece_rows)
    starts = ends - piece_rows
    row_steps = jnp.arange(rows, dtype=jnp.int32)
    segment = jnp.sum((row_steps[:, None] >= ends[None, :]).astype(jnp.int32), axis=1)
    member = segment[:, None] == jnp.arange(piece_units.shape[0], dtype=jnp.int32)[None, :]
    row_start = jnp.sum(jnp.where(member, starts[None, :], 0), axis=1)
    positions = (row_steps - row_start).astype(jnp.float32)
    keep = (segment < piece_units.shape[0] - 1).astype(jnp.float32)
    return (segment, row_steps, positions, keep)


def permitted(block_segment, block_steps, segment, row_steps):
    return (block_segment[:, None] == segment[None, :]) & (
        row_steps[None, :] <= block_steps[:, None]
    )


def spread_rows(values):
    return lax.all_gather(values, "tensor", axis=0, tiled=True)


def spread_grads(values):
    return lax.all_gather(values, "tensor", axis=0, tiled=True)


def per_device(
    tokens,
    lengths,
    gain_attn,
    w_query,
    w_kv,
    w_attn_out,
    gain_mlp,
    w_gate,
    w_up,
    w_down,
    out_grad,
    kv_grad,
):
    local_rows = tokens.shape[0]
    parts = lax.axis_size("tensor")
    total_rows = local_rows * parts
    first_row = lax.axis_index("tensor") * local_rows
    segment, row_steps, positions, keep = layout(lengths[0], total_rows)
    head_dim = w_kv.shape[1] // 2
    local_heads = w_query.shape[1] // head_dim
    scale = head_dim ** (-0.5)
    cosine, sine = rotary_tables(positions, head_dim)
    row_keep = lax.dynamic_slice_in_dim(keep, first_row, local_rows, 0)[:, None]
    row_cosine = lax.dynamic_slice_in_dim(cosine, first_row, local_rows, 0)
    row_sine = lax.dynamic_slice_in_dim(sine, first_row, local_rows, 0)
    tokens_full = tokens.astype(jnp.float32)
    inv_first = lax.rsqrt(jnp.mean(tokens_full * tokens_full, axis=-1, keepdims=True) + EPSILON)
    unit_first = tokens_full * inv_first
    normed_rows = (unit_first * gain_attn).astype(jnp.bfloat16)
    normed = spread_rows(normed_rows)
    queries = jnp.dot(normed, w_query, preferred_element_type=jnp.float32).reshape(
        total_rows, local_heads, head_dim
    )
    queries = rotate(queries, cosine[:, None, :], sine[:, None, :]).astype(jnp.bfloat16)
    kv_raw = jnp.dot(normed, w_kv, preferred_element_type=jnp.float32)
    shared = jnp.concatenate(
        [rotate(kv_raw[:, :head_dim], cosine, sine), kv_raw[:, head_dim:]], axis=1
    ).astype(jnp.bfloat16)
    keys = shared[:, :head_dim]
    values = shared[:, head_dim:]
    block = min(512, total_rows)
    count = total_rows // block
    pieces = []
    log_totals = []
    for number in range(count):
        begin = number * block
        query_block = queries[begin : begin + block]
        allowed = permitted(
            segment[begin : begin + block], row_steps[begin : begin + block], segment, row_steps
        )
        scores = (
            jnp.einsum("qhd,kd->hqk", query_block, keys, preferred_element_type=jnp.float32) * scale
        )
        scores = jnp.where(allowed[None], scores, MASKED)
        row_max = jnp.max(scores, axis=-1, keepdims=True)
        exp_scores = jnp.exp(scores - row_max)
        row_total = jnp.sum(exp_scores, axis=-1, keepdims=True)
        log_totals.append(row_max + jnp.log(row_total))
        weights = (exp_scores / row_total).astype(jnp.bfloat16)
        pieces.append(
            jnp.einsum("hqk,kd->qhd", weights, values, preferred_element_type=jnp.float32).astype(
                jnp.bfloat16
            )
        )
    attended = jnp.concatenate(pieces, axis=0).reshape(total_rows, local_heads * head_dim)
    attn_rows = lax.psum_scatter(
        jnp.dot(attended, w_attn_out, preferred_element_type=jnp.float32).astype(jnp.bfloat16),
        "tensor",
        scatter_dimension=0,
        tiled=True,
    ).astype(jnp.float32)
    mid = tokens_full + attn_rows
    inv_second = lax.rsqrt(jnp.mean(mid * mid, axis=-1, keepdims=True) + EPSILON)
    unit_second = mid * inv_second
    normed_mlp = spread_rows((unit_second * gain_mlp).astype(jnp.bfloat16))
    gate = jnp.dot(normed_mlp, w_gate, preferred_element_type=jnp.float32)
    up = jnp.dot(normed_mlp, w_up, preferred_element_type=jnp.float32)
    sigma = jax.nn.sigmoid(gate)
    active = gate * sigma
    hidden = (active * up).astype(jnp.bfloat16)
    mlp_rows = lax.psum_scatter(
        jnp.dot(hidden, w_down, preferred_element_type=jnp.float32).astype(jnp.bfloat16),
        "tensor",
        scatter_dimension=0,
        tiled=True,
    ).astype(jnp.float32)
    block_out = (row_keep * (mid + mlp_rows)).astype(jnp.bfloat16)
    out_full = row_keep * out_grad.astype(jnp.float32)
    grad_mlp = spread_grads(out_full.astype(jnp.bfloat16))
    g_down = jnp.einsum("rf,rd->fd", hidden, grad_mlp, preferred_element_type=jnp.float32)
    g_hidden = jnp.einsum("rd,fd->rf", grad_mlp, w_down, preferred_element_type=jnp.float32)
    d_gate = (g_hidden * up * sigma * (1.0 + gate * (1.0 - sigma))).astype(jnp.bfloat16)
    d_up = (g_hidden * active).astype(jnp.bfloat16)
    g_gate = jnp.einsum("rd,rf->df", normed_mlp, d_gate, preferred_element_type=jnp.float32)
    g_up = jnp.einsum("rd,rf->df", normed_mlp, d_up, preferred_element_type=jnp.float32)
    back_mlp = lax.psum_scatter(
        (
            jnp.einsum("rf,df->rd", d_gate, w_gate, preferred_element_type=jnp.float32)
            + jnp.einsum("rf,df->rd", d_up, w_up, preferred_element_type=jnp.float32)
        ).astype(jnp.bfloat16),
        "tensor",
        scatter_dimension=0,
        tiled=True,
    ).astype(jnp.float32)
    e_mlp = back_mlp * gain_mlp
    g_gain_mlp = jnp.sum(back_mlp * unit_second, axis=0)
    d_mid = out_full + inv_second * (
        e_mlp - unit_second * jnp.mean(e_mlp * unit_second, axis=-1, keepdims=True)
    )
    grad_attn = spread_grads(d_mid.astype(jnp.bfloat16))
    g_attn_out = jnp.einsum("rh,rd->hd", attended, grad_attn, preferred_element_type=jnp.float32)
    d_att = jnp.einsum(
        "rd,hd->rh", grad_attn, w_attn_out, preferred_element_type=jnp.float32
    ).astype(jnp.bfloat16)
    d_att = d_att.reshape(total_rows, local_heads, head_dim)
    query_pieces = []
    d_keys = jnp.zeros((total_rows, head_dim), jnp.float32)
    d_values = jnp.zeros((total_rows, head_dim), jnp.float32)
    for number in range(count):
        begin = number * block
        query_block = queries[begin : begin + block]
        grad_block = d_att[begin : begin + block]
        allowed = permitted(
            segment[begin : begin + block], row_steps[begin : begin + block], segment, row_steps
        )
        scores = (
            jnp.einsum("qhd,kd->hqk", query_block, keys, preferred_element_type=jnp.float32) * scale
        )
        scores = jnp.where(allowed[None], scores, MASKED)
        probs = jnp.exp(scores - log_totals[number])
        weights = probs.astype(jnp.bfloat16)
        d_probs = jnp.einsum("qhd,kd->hqk", grad_block, values, preferred_element_type=jnp.float32)
        inner = jnp.sum(d_probs * probs, axis=-1, keepdims=True)
        d_scores = (probs * (d_probs - inner)).astype(jnp.bfloat16)
        query_pieces.append(
            jnp.einsum("hqk,kd->qhd", d_scores, keys, preferred_element_type=jnp.float32) * scale
        )
        d_keys = (
            d_keys
            + jnp.einsum("hqk,qhd->kd", d_scores, query_block, preferred_element_type=jnp.float32)
            * scale
        )
        d_values = d_values + jnp.einsum(
            "hqk,qhd->kd", weights, grad_block, preferred_element_type=jnp.float32
        )
    d_queries = jnp.concatenate(query_pieces, axis=0)
    d_queries = unrotate(d_queries, cosine[:, None, :], sine[:, None, :]).astype(jnp.bfloat16)
    d_queries = d_queries.reshape(total_rows, local_heads * head_dim)
    g_query = jnp.einsum("rd,rh->dh", normed, d_queries, preferred_element_type=jnp.float32)
    kv_rows = lax.psum_scatter(
        jnp.concatenate([d_keys, d_values], axis=1).astype(jnp.bfloat16),
        "tensor",
        scatter_dimension=0,
        tiled=True,
    ).astype(jnp.float32)
    kv_rows = kv_rows + row_keep * kv_grad.astype(jnp.float32)
    d_kv = jnp.concatenate(
        [unrotate(kv_rows[:, :head_dim], row_cosine, row_sine), kv_rows[:, head_dim:]], axis=1
    ).astype(jnp.bfloat16)
    g_kv = jnp.einsum("rd,rk->dk", normed_rows, d_kv, preferred_element_type=jnp.float32)
    back_attn = lax.psum_scatter(
        jnp.einsum("rh,dh->rd", d_queries, w_query, preferred_element_type=jnp.float32).astype(
            jnp.bfloat16
        ),
        "tensor",
        scatter_dimension=0,
        tiled=True,
    ).astype(jnp.float32)
    back_attn = back_attn + jnp.einsum("rk,dk->rd", d_kv, w_kv, preferred_element_type=jnp.float32)
    e_attn = back_attn * gain_attn
    g_gain_attn = jnp.sum(back_attn * unit_first, axis=0)
    grad_tokens = (
        d_mid
        + inv_first * (e_attn - unit_first * jnp.mean(e_attn * unit_first, axis=-1, keepdims=True))
    ).astype(jnp.bfloat16)
    kv_sum, gain_sums = (
        lax.psum_scatter(g_kv, ("dp", "tensor"), scatter_dimension=0, tiled=True),
        lax.psum_scatter(
            jnp.stack([g_gain_attn, g_gain_mlp]), ("dp", "tensor"), scatter_dimension=1, tiled=True
        ),
    )
    query_sum, out_sum, gate_sum, up_sum, down_sum = (
        lax.psum_scatter(
            g_query.astype(jnp.bfloat16), "dp", scatter_dimension=0, tiled=True
        ).astype(jnp.float32),
        lax.psum_scatter(
            g_attn_out.astype(jnp.bfloat16), "dp", scatter_dimension=1, tiled=True
        ).astype(jnp.float32),
        lax.psum_scatter(g_gate.astype(jnp.bfloat16), "dp", scatter_dimension=0, tiled=True).astype(
            jnp.float32
        ),
        lax.psum_scatter(g_up.astype(jnp.bfloat16), "dp", scatter_dimension=0, tiled=True).astype(
            jnp.float32
        ),
        lax.psum_scatter(g_down.astype(jnp.bfloat16), "dp", scatter_dimension=1, tiled=True).astype(
            jnp.float32
        ),
    )
    return (
        block_out,
        grad_tokens,
        gain_sums[0],
        query_sum,
        kv_sum,
        out_sum,
        gain_sums[1],
        gate_sum,
        up_sum,
        down_sum,
    )


def solution(mesh):
    placed = (
        P(("dp", "tensor"), None),
        P("dp", None),
        P(),
        P(None, "tensor"),
        P(),
        P("tensor", None),
        P(),
        P(None, "tensor"),
        P(None, "tensor"),
        P("tensor", None),
        P(("dp", "tensor"), None),
        P(("dp", "tensor"), None),
    )
    return jax.shard_map(
        per_device,
        mesh=mesh,
        in_specs=placed,
        out_specs=(
            P(("dp", "tensor"), None),
            P(("dp", "tensor"), None),
            P(("dp", "tensor")),
            P("dp", "tensor"),
            P(("dp", "tensor"), None),
            P("tensor", "dp"),
            P(("dp", "tensor")),
            P("dp", "tensor"),
            P("dp", "tensor"),
            P("tensor", "dp"),
        ),
        check_vma=False,
    )
```

profile of v0, /device:TPU:0, one launch (start us, length us, event | category | flops | bytes accessed | tf_op | source)
XLA Modules:
  0.0 1251.9 jit_solution(9932301700747642198)
XLA Ops:
  14.4 72.6 %all-gather.5.cloned.1.call-done = bf16[1024,2048]{1,0:T(8,128)(2,1)} async-done(((bf16[128,2048]{1,0:T(8,128)(2,1)}), bf16[1024,2048]{1,0:T(8,128)(2,1)}) %all-gather.5.cloned.1.call-update) | async-done | bytes 4194320 | tf_op jit(solution)/shard_map/all_gather | solution.py:61
  86.9 3.8 fusion.81
  95.5 3.8 fusion.82
  119.2 85.8 %reduce-scatter.17.cloned.1.call-done = bf16[128,2048]{1,0:T(8,128)(2,1)} async-done(((bf16[1024,2048]{1,0:T(8,128)(2,1)}), bf16[128,2048]{1,0:T(8,128)(2,1)}) %reduce-scatter.17.cloned.1.call-update) | async-done | bytes 524304 | tf_op jit(solution)/shard_map/reduce_scatter | solution.py:134
  210.6 71.1 %all-gather.7.cloned.1.call-done = bf16[1024,2048]{1,0:T(8,128)(2,1)} async-done(((bf16[128,2048]{1,0:T(8,128)(2,1)}), bf16[1024,2048]{1,0:T(8,128)(2,1)}) %all-gather.7.cloned.1.call-update) | async-done | bytes 4194320 | tf_op jit(solution)/shard_map/all_gather | solution.py:61
  281.7 8.0 fusion.84
  289.7 4.7 fusion.83
  294.4 61.7 %all-gather.9.cloned.1.call-done = bf16[1024,2048]{1,0:T(8,128)(2,1)} async-done(((bf16[128,2048]{1,0:T(8,128)(2,1)}), bf16[1024,2048]{1,0:T(8,128)(2,1)}) %all-gather.9.cloned.1.call-update) | async-done | bytes 4194320 | tf_op jit(solution)/shard_map/all_gather | solution.py:65
  356.2 8.4 multiply_convert_fusion
  364.6 3.5 fusion.85
  368.2 5.4 add_convert_fusion
  373.7 86.4 %reduce-scatter.21.cloned.1.call-done = bf16[128,2048]{1,0:T(8,128)(2,1)} async-done(((bf16[1024,2048]{1,0:T(8,128)(2,1)}), bf16[128,2048]{1,0:T(8,128)(2,1)}) %reduce-scatter.21.cloned.1.call-update) | async-done | bytes 524304 | tf_op jit(solution)/shard_map/reduce_scatter | solution.py:164
  467.2 71.7 %all-gather.11.cloned.1.call-done = bf16[1024,2048]{1,0:T(8,128)(2,1)} async-done(((bf16[128,2048]{1,0:T(8,128)(2,1)}), bf16[1024,2048]{1,0:T(8,128)(2,1)}) %all-gather.11.cloned.1.call-update) | async-done | bytes 4194320 | tf_op jit(solution)/shard_map/all_gather | solution.py:65
  538.9 3.9 convolution_convert_fusion.8
  564.9 4.7 convolution_convert_fusion
  569.7 7.4 convolution_convert_fusion.5
  577.1 7.5 convolution_convert_fusion.3
  584.7 7.4 convolution_convert_fusion.4
  592.2 4.6 convolution_convert_fusion.6
  597.1 4.6 convolution_convert_fusion.7
  601.8 6.4 convolution_convert_fusion.1
  609.2 7.8 reduce-scatter.37.cloned.1.call-done
  619.4 88.8 %reduce-scatter.23.cloned.1.call-done = bf16[128,2048]{1,0:T(8,128)(2,1)} async-done(((bf16[1024,2048]{1,0:T(8,128)(2,1)}), bf16[128,2048]{1,0:T(8,128)(2,1)}) %reduce-scatter.23.cloned.1.call-update) | async-done | bytes 524304 | tf_op jit(solution)/shard_map/reduce_scatter | solution.py:229
  716.4 30.5 %reduce-scatter.35.cloned.1.call-done = bf16[704,512]{1,0:T(8,128)(2,1)} async-done(((bf16[704,2048]{1,0:T(8,128)(2,1)}), bf16[704,512]{1,0:T(8,128)(2,1)}) %reduce-scatter.35.cloned.1.call-update) | async-done | bytes 720912 | tf_op jit(solution)/shard_map/reduce_scatter | solution.py:263
  749.3 36.5 %reduce-scatter.33.cloned.1.call-done = bf16[512,704]{0,1:T(8,128)(2,1)} async-done(((bf16[2048,704]{0,1:T(8,128)(2,1)}), bf16[512,704]{0,1:T(8,128)(2,1)}) %reduce-scatter.33.cloned.1.call-update) | async-done | bytes 720912 | tf_op jit(solution)/shard_map/reduce_scatter | solution.py:260
  788.1 36.5 %reduce-scatter.31.cloned.1.call-done = bf16[512,704]{0,1:T(8,128)(2,1)} async-done(((bf16[2048,704]{0,1:T(8,128)(2,1)}), bf16[512,704]{0,1:T(8,128)(2,1)}) %reduce-scatter.31.cloned.1.call-update) | async-done | bytes 720912 | tf_op jit(solution)/shard_map/reduce_scatter | solution.py:257
  827.1 25.0 %reduce-scatter.29.cloned.1.call-done = bf16[256,512]{1,0:T(8,128)(2,1)} async-done(((bf16[256,2048]{1,0:T(8,128)(2,1)}), bf16[256,512]{1,0:T(8,128)(2,1)}) %reduce-scatter.29.cloned.1.call-update) | async-done | bytes 262160 | tf_op jit(solution)/shard_map/reduce_scatter | solution.py:254
  853.9 25.6 %reduce-scatter.25.cloned.1.call-done = bf16[512,256]{1,0:T(8,128)(2,1)} async-done(((bf16[2048,256]{1,0:T(8,128)(2,1)}), bf16[512,256]{1,0:T(8,128)(2,1)}) %reduce-scatter.25.cloned.1.call-update) | async-done | bytes 262160 | tf_op jit(solution)/shard_map/reduce_scatter | solution.py:251
  881.3 90.1 %reduce-scatter.19.cloned.1.call-done = bf16[128,2048]{1,0:T(8,128)(2,1)} async-done(((bf16[1024,2048]{1,0:T(8,128)(2,1)}), bf16[128,2048]{1,0:T(8,128)(2,1)}) %reduce-scatter.19.cloned.1.call-update) | async-done | bytes 524304 | tf_op jit(solution)/shard_map/reduce_scatter | solution.py:149
  971.4 3.8 fusion.57
  975.2 133.1 %reduce-scatter.39.cloned.1.call-done = f32[64,2]{1,0:T(8,128)} async-done(((f32[2048,2]{1,0:T(8,128)}), f32[64,2]{1,0:T(8,128)}) %reduce-scatter.39.cloned.1.call-update) | async-done | bytes 528
  1110.3 134.6 %reduce-scatter.27.cloned.1.call-done = f32[64,256]{1,0:T(8,128)} async-done(((f32[2048,256]{1,0:T(8,128)}), f32[64,256]{1,0:T(8,128)}) %reduce-scatter.27.cloned.1.call-update) | async-done | bytes 65552 | tf_op jit(solution)/shard_map/reduce_scatter | solution.py:245
  (201 shorter events, 91.2 us)
Async XLA Ops:
  7.2 349.0 %copy-start = (bf16[704,2048]{1,0:T(8,128)(2,1)S(1)}, bf16[704,2048]{1,0:T(8,128)(2,1)}, u32[]{:S(2)}) copy-start(bf16[704,2048]{1,0:T(8,128)(2,1)} %param.21) | copy-start | bytes 8650756
  7.2 79.7 %all-gather.5.cloned.1.call-start = ((), (), s32[]{:S(2)}) async-start(), calls=%async_computation.12 | async-start | bytes 4718592 | tf_op jit(solution)/shard_map/all_gather | solution.py:61
  10.7 194.3 %reduce-scatter.17.cloned.1.call-start = ((), (), s32[]{:S(2)}) async-start(), calls=%async_computation.13 | async-start | bytes 4718592 | tf_op jit(solution)/shard_map/reduce_scatter | solution.py:134
  93.5 5.8 copy-start.18
  93.5 5.8 copy-start.19
  115.4 89.6 %copy-start.5 = (bf16[128,2048]{1,0:T(8,128)(2,1)S(1)}, bf16[128,2048]{1,0:T(8,128)(2,1)}, u32[]{:S(2)}) copy-start(bf16[128,2048]{1,0:T(8,128)(2,1)} %param.12) | copy-start | bytes 1572868
  118.7 87.6 %copy-start.24 = (f32[2048]{0:T(1024)S(1)}, f32[2048]{0:T(1024)}, u32[]{:S(2)}) copy-start(f32[2048]{0:T(1024)} %param.18) | copy-start | bytes 24580
  118.7 163.0 %all-gather.7.cloned.1.call-start = ((), (), s32[]{:S(2)}) async-start(), calls=%async_computation.14 | async-start | bytes 4718592 | tf_op jit(solution)/shard_map/all_gather | solution.py:61
  206.3 256.2 %copy-start.32 = (f32[128]{0:T(128)}, f32[128]{0:T(128)S(1)}, u32[]{:S(2)}) copy-start(f32[128]{0:T(128)S(1)} %add_rsqrt_fusion) | copy-start | bytes 1540
  208.4 147.8 %all-gather.9.cloned.1.call-start = ((), (), s32[]{:S(2)}) async-start(), calls=%async_computation.16 | async-start | bytes 4718592 | tf_op jit(solution)/shard_map/all_gather | solution.py:65
  208.5 81.2 %copy-start.34 = (f32[128]{0:T(128)}, f32[128]{0:T(128)S(1)}, u32[]{:S(2)}) copy-start(f32[128]{0:T(128)S(1)} %dynamic_slice.9) | copy-start | bytes 1540
  210.5 249.6 %reduce-scatter.21.cloned.1.call-start = ((), (), s32[]{:S(2)}) async-start(), calls=%async_computation.17 | async-start | bytes 4718592 | tf_op jit(solution)/shard_map/reduce_scatter | solution.py:164
  281.7 8.0 copy-start.40
  281.7 8.0 copy-start.41
  356.2 8.5 copy-start.42
  373.6 92.2 %copy-start.29 = (f32[2,512]{1,0:T(2,128)S(1)}, f32[2,512]{1,0:T(2,128)}, u32[]{:S(2)}) copy-start(f32[2,512]{1,0:T(2,128)} %copy-done.28) | copy-start | bytes 12292
  373.7 165.2 %all-gather.11.cloned.1.call-start = ((), (), s32[]{:S(2)}) async-start(), calls=%async_computation.18 | async-start | bytes 4718592 | tf_op jit(solution)/shard_map/all_gather | solution.py:65
  465.6 151.3 %reduce-scatter.37.cloned.1.call-start = ((), (), s32[]{:S(2)}) async-start(), calls=%async_computation.26 | async-start | bytes 589824
  556.6 151.5 %reduce-scatter.23.cloned.1.call-start = ((), (), s32[]{:S(2)}) async-start(), calls=%async_computation.19 | async-start | bytes 4718592 | tf_op jit(solution)/shard_map/reduce_scatter | solution.py:229
  569.6 177.3 %reduce-scatter.35.cloned.1.call-start = ((), (), s32[]{:S(2)}) async-start(), calls=%async_computation.25 | async-start | bytes 3604480 | tf_op jit(solution)/shard_map/reduce_scatter | solution.py:263
  577.1 208.6 %reduce-scatter.33.cloned.1.call-start = ((), (), s32[]{:S(2)}) async-start(), calls=%async_computation.24 | async-start | bytes 3604480 | tf_op jit(solution)/shard_map/reduce_scatter | solution.py:260
  584.6 240.0 %reduce-scatter.31.cloned.1.call-start = ((), (), s32[]{:S(2)}) async-start(), calls=%async_computation.23 | async-start | bytes 3604480 | tf_op jit(solution)/shard_map/reduce_scatter | solution.py:257
  592.1 260.0 %reduce-scatter.29.cloned.1.call-start = ((), (), s32[]{:S(2)}) async-start(), calls=%async_computation.22 | async-start | bytes 1310720 | tf_op jit(solution)/shard_map/reduce_scatter | solution.py:254
  596.8 282.8 %reduce-scatter.25.cloned.1.call-start = ((), (), s32[]{:S(2)}) async-start(), calls=%async_computation.20 | async-start | bytes 1310720 | tf_op jit(solution)/shard_map/reduce_scatter | solution.py:251
  601.7 369.7 %reduce-scatter.19.cloned.1.call-start = ((), (), s32[]{:S(2)}) async-start(), calls=%async_computation.15 | async-start | bytes 4718592 | tf_op jit(solution)/shard_map/reduce_scatter | solution.py:149
  608.2 100.0 %copy-start.25 = (f32[2048]{0:T(1024)S(1)}, f32[2048]{0:T(1024)}, u32[]{:S(2)}) copy-start(f32[2048]{0:T(1024)} %param.14) | copy-start | bytes 24580
  608.2 500.0 %reduce-scatter.39.cloned.1.call-start = ((), (), s32[]{:S(2)}) async-start(), calls=%async_computation.27 | async-start | bytes 1081344
  713.4 531.5 %reduce-scatter.27.cloned.1.call-start = ((), (), s32[]{:S(2)}) async-start(), calls=%async_computation.21 | async-start | bytes 2162688 | tf_op jit(solution)/shard_map/reduce_scatter | solution.py:245
  716.3 255.1 %copy-start.33 = (f32[128]{0:T(128)S(1)}, f32[128]{0:T(128)}, u32[]{:S(2)}) copy-start(f32[128]{0:T(128)} %copy-done.32) | copy-start | bytes 1540
  716.3 255.1 %copy-start.35 = (f32[128]{0:T(128)S(1)}, f32[128]{0:T(128)}, u32[]{:S(2)}) copy-start(f32[128]{0:T(128)} %copy-done.34) | copy-start | bytes 1540
  716.3 255.1 %copy-start.37 = (f32[128]{0:T(128)S(1)}, f32[128]{0:T(128)}, u32[]{:S(2)}) copy-start(f32[128]{0:T(128)} %copy-done.36) | copy-start | bytes 1540
  716.4 255.1 %copy-start.39 = (f32[128]{0:T(128)S(1)}, f32[128]{0:T(128)}, u32[]{:S(2)}) copy-start(f32[128]{0:T(128)} %copy-done.38) | copy-start | bytes 1540
  (30 other events, 69.4 us)
Sparse Core Ops, SparseCore 0:
  10.8 76.0 all-gather.4
  118.8 86.1 reduce-scatter.16
  208.5 73.1 all-gather.6
  284.5 71.6 all-gather.8
  373.8 86.3 reduce-scatter.20
  465.7 73.1 all-gather.10
  556.8 60.1 reduce-scatter.36
  621.0 87.1 reduce-scatter.22
  710.7 36.0 reduce-scatter.34
  749.4 36.2 reduce-scatter.32
  788.3 36.3 reduce-scatter.30
  827.2 24.8 reduce-scatter.28
  854.6 24.8 reduce-scatter.24
  883.5 87.8 reduce-scatter.18
  973.5 134.7 reduce-scatter.38
  1111.0 133.8 reduce-scatter.26
where the time goes:
time: 1260 us; the launch traced here: 1250 us
  waiting for transfers between devices  1060 us (84%)
  matrix products  108 us (9%)
  other arithmetic  47.2 us (4%)
  local copies, waits for them, and re-layouts  22 us (2%)
  between operations  15 us (1%)
    all_gather x2, waiting for transfers between devices, spread_rows(): return lax.all_gather(values, 'tensor', axis=0, tiled=True)  144 us
    unnamed x18, waiting for transfers between devices  141 us
    reduce_scatter x1, waiting for transfers between devices, per_device(): lax.psum_scatter(g_kv, ('dp', 'tensor'), scatter_dimension=0, tiled=True)  135 us
    all_gather x2, waiting for transfers between devices, spread_grads(): return lax.all_gather(values, 'tensor', axis=0, tiled=True)  133 us
    reduce_scatter x1, waiting for transfers between devices, per_device(): lax.psum_scatter(jnp.dot(hidden, w_down, preferred_element_type=jnp.float...  90.1 us
    reduce_scatter x1, waiting for transfers between devices, per_device(): lax.psum_scatter(jnp.einsum('rh,dh->rd', d_queries, w_query, preferred_el...  88.8 us
    reduce_scatter x1, waiting for transfers between devices, per_device(): lax.psum_scatter((jnp.einsum('rf,df->rd', d_gate, w_gate, preferred_eleme...  86.4 us
    reduce_scatter x1, waiting for transfers between devices, per_device(): lax.psum_scatter(jnp.dot(attended, w_attn_out, preferred_element_type=jnp...  85.8 us
  transfers between devices with their start and end apart: 16, of which 16 were waited for; matrix products, arithmetic and copies ran while one was open for 8% of the time, Pallas kernels for 0%

commit v1 on v0

--- a/solution.py
+++ b/solution.py
@@ -225,7 +225,16 @@
     d_kv = jnp.concatenate(
         [unrotate(kv_rows[:, :head_dim], row_cosine, row_sine), kv_rows[:, head_dim:]], axis=1
     ).astype(jnp.bfloat16)
-    g_kv = jnp.einsum("rd,rk->dk", normed_rows, d_kv, preferred_element_type=jnp.float32)
+    d_kv_all = lax.all_gather(d_kv, "tensor", axis=0, tiled=True)
+    width = normed.shape[1]
+    groups = lax.axis_size("dp")
+    own = lax.dynamic_index_in_dim(
+        normed.reshape(total_rows, groups, parts, width // (groups * parts)),
+        lax.axis_index("tensor"),
+        2,
+        False,
+    ).reshape(total_rows, width // parts)
+    g_kv = jnp.einsum("rd,rk->dk", own, d_kv_all, preferred_element_type=jnp.float32)
     back_attn = lax.psum_scatter(
         jnp.einsum("rh,dh->rd", d_queries, w_query, preferred_element_type=jnp.float32).astype(
             jnp.bfloat16
@@ -241,12 +250,11 @@
         d_mid
         + inv_first * (e_attn - unit_first * jnp.mean(e_attn * unit_first, axis=-1, keepdims=True))
     ).astype(jnp.bfloat16)
-    kv_sum, gain_sums = (
-        lax.psum_scatter(g_kv, ("dp", "tensor"), scatter_dimension=0, tiled=True),
-        lax.psum_scatter(
-            jnp.stack([g_gain_attn, g_gain_mlp]), ("dp", "tensor"), scatter_dimension=1, tiled=True
-        ),
-    )
+    kv_sum = lax.psum_scatter(g_kv, "dp", scatter_dimension=0, tiled=True)
+    share = width // (groups * parts)
+    first = (lax.axis_index("dp") * parts + lax.axis_index("tensor")) * share
+    gain_all = lax.all_gather(jnp.stack([g_gain_attn, g_gain_mlp]), ("dp", "tensor"), axis=0)
+    gain_sums = jnp.sum(lax.dynamic_slice_in_dim(gain_all, first, share, 2), axis=0)
     query_sum, out_sum, gate_sum, up_sum, down_sum = (
         lax.psum_scatter(
             g_query.astype(jnp.bfloat16), "dp", scatter_dimension=0, tiled=True

time: 1260 us -> 1000 us (0.79)
  waiting for transfers between devices: 1060 us -> 684 us
  blocking collectives: 0 us -> 101 us
    reduce_scatter x1, waiting for transfers between devices: 135 us -> 18.9 us  [per_device(): kv_sum = lax.psum_scatter(g_kv, 'dp', scatter_dimension=0, tiled=True)]
    all_gather x0 -> x2, blocking collectives: none -> 101 us  [the longest x1 73.9 us: per_device(): lax.all_gather(jnp.stack([g_gain_attn, g_gain_mlp]), ('dp', 'tensor'), ax...]
    unnamed x18 -> x16, waiting for transfers between devices: 141 us -> 63.9 us
    reduce_scatter x1, waiting for transfers between devices: 90.1 us -> 18.5 us  [per_device(): lax.psum_scatter(jnp.dot(hidden, w_down, preferred_element_type=jnp.float...]
    all_gather x2, waiting for transfers between devices: 133 us -> 102 us  [spread_grads(): return lax.all_gather(values, 'tensor', axis=0, tiled=True)]
    reduce_scatter x1, waiting for transfers between devices: 30.5 us -> 0.01 us  [per_device(): lax.psum_scatter(g_down.astype(jnp.bfloat16), 'dp', scatter_dimension=1,...]
    reduce_scatter x1, waiting for transfers between devices: 25 us -> 0.02 us  [per_device(): lax.psum_scatter(g_attn_out.astype(jnp.bfloat16), 'dp', scatter_dimension...]
    reduce_scatter x1, waiting for transfers between devices: 36.5 us -> 18.5 us  [per_device(): lax.psum_scatter(g_up.astype(jnp.bfloat16), 'dp', scatter_dimension=0, ti...]
  transfers between devices with their start and end apart: 16 -> 15, of which waited for: 16 -> 13; matrix products, arithmetic and copies ran while one was open for 8% -> 12% of each run, Pallas kernels for 0% -> 0%
where the time goes in v1:
time: 1000 us; the launch traced here: 992 us
  waiting for transfers between devices  684 us (68%)
  matrix products  108 us (11%)
  blocking collectives  101 us (10%)
  other arithmetic  44.8 us (4%)
  local copies, waits for them, and re-layouts  28.2 us (3%)
  between operations  15 us (2%)
  starting transfers between devices  10.8 us (1%)
    all_gather x2, waiting for transfers between devices, spread_rows(): return lax.all_gather(values, 'tensor', axis=0, tiled=True)  144 us
    all_gather x2, waiting for transfers between devices, spread_grads(): return lax.all_gather(values, 'tensor', axis=0, tiled=True)  102 us
    reduce_scatter x1, waiting for transfers between devices, per_device(): lax.psum_scatter(jnp.einsum('rh,dh->rd', d_queries, w_query, preferred_el...  89.8 us
    reduce_scatter x1, waiting for transfers between devices, per_device(): lax.psum_scatter((jnp.einsum('rf,df->rd', d_gate, w_gate, preferred_eleme...  86.4 us
    reduce_scatter x1, waiting for transfers between devices, per_device(): lax.psum_scatter(jnp.dot(attended, w_attn_out, preferred_element_type=jnp...  86 us
    all_gather x1, blocking collectives, per_device(): lax.all_gather(jnp.stack([g_gain_attn, g_gain_mlp]), ('dp', 'tensor'), ax...  73.9 us
    unnamed x16, waiting for transfers between devices  63.9 us
    reduce_scatter x1, waiting for transfers between devices, per_device(): lax.psum_scatter(g_gate.astype(jnp.bfloat16), 'dp', scatter_dimension=0,...  36.5 us
  transfers between devices with their start and end apart: 15, of which 13 were waited for; matrix products, arithmetic and copies ran while one was open for 12% of the time, Pallas kernels for 0%

profile of v1, /device:TPU:0, one launch (start us, length us, event | category | flops | bytes accessed | tf_op | source)
XLA Modules:
  0.0 991.8 jit_solution(8764303690428286857)
XLA Ops:
  14.3 72.6 %all-gather.7.cloned.1.call-done = bf16[1024,2048]{1,0:T(8,128)(2,1)} async-done(((bf16[128,2048]{1,0:T(8,128)(2,1)}), bf16[1024,2048]{1,0:T(8,128)(2,1)}) %all-gather.7.cloned.1.call-update) | async-done | bytes 4194320 | tf_op jit(solution)/shard_map/all_gather | solution.py:61
  86.9 3.8 fusion.77
  95.5 3.8 fusion.78
  119.0 86.0 %reduce-scatter.14.cloned.1.call-done = bf16[128,2048]{1,0:T(8,128)(2,1)} async-done(((bf16[1024,2048]{1,0:T(8,128)(2,1)}), bf16[128,2048]{1,0:T(8,128)(2,1)}) %reduce-scatter.14.cloned.1.call-update) | async-done | bytes 524304 | tf_op jit(solution)/shard_map/reduce_scatter | solution.py:134
  211.1 71.1 %all-gather.9.cloned.1.call-done = bf16[1024,2048]{1,0:T(8,128)(2,1)} async-done(((bf16[128,2048]{1,0:T(8,128)(2,1)}), bf16[1024,2048]{1,0:T(8,128)(2,1)}) %all-gather.9.cloned.1.call-update) | async-done | bytes 4194320 | tf_op jit(solution)/shard_map/all_gather | solution.py:61
  282.2 8.0 fusion.80
  290.2 4.7 fusion.79
  295.0 61.7 %all-gather.11.cloned.1.call-done = bf16[1024,2048]{1,0:T(8,128)(2,1)} async-done(((bf16[128,2048]{1,0:T(8,128)(2,1)}), bf16[1024,2048]{1,0:T(8,128)(2,1)}) %all-gather.11.cloned.1.call-update) | async-done | bytes 4194320 | tf_op jit(solution)/shard_map/all_gather | solution.py:65
  356.7 8.4 multiply_convert_fusion
  368.7 5.4 add_convert_fusion
  374.2 86.4 %reduce-scatter.18.cloned.1.call-done = bf16[128,2048]{1,0:T(8,128)(2,1)} async-done(((bf16[1024,2048]{1,0:T(8,128)(2,1)}), bf16[128,2048]{1,0:T(8,128)(2,1)}) %reduce-scatter.18.cloned.1.call-update) | async-done | bytes 524304 | tf_op jit(solution)/shard_map/reduce_scatter | solution.py:164
  466.1 7.3 convolution_convert_fusion.5
  473.5 9.7 reduce-scatter.30.cloned.1.call-start
  483.3 7.4 convolution_convert_fusion.3
  490.7 7.3 convolution_convert_fusion.4
  499.5 39.9 %all-gather.13.cloned.1.call-done = bf16[1024,2048]{1,0:T(8,128)(2,1)} async-done(((bf16[128,2048]{1,0:T(8,128)(2,1)}), bf16[1024,2048]{1,0:T(8,128)(2,1)}) %all-gather.13.cloned.1.call-update) | async-done | bytes 4194320 | tf_op jit(solution)/shard_map/all_gather | solution.py:65
  539.4 3.9 convolution_convert_fusion.8
  555.6 4.6 convolution_convert_fusion.6
  569.4 4.6 convolution_convert_fusion.7
  574.1 4.8 convolution_convert_fusion
  578.9 6.4 convolution_convert_fusion.1
  586.3 6.6 copy.119
  597.2 18.5 %reduce-scatter.30.cloned.1.call-done = bf16[512,704]{0,1:T(8,128)(2,1)} async-done(((bf16[2048,704]{0,1:T(8,128)(2,1)}), bf16[512,704]{0,1:T(8,128)(2,1)}) %reduce-scatter.30.cloned.1.call-update) | async-done | bytes 720912 | tf_op jit(solution)/shard_map/reduce_scatter | solution.py:268
  618.1 36.5 %reduce-scatter.28.cloned.1.call-done = bf16[512,704]{0,1:T(8,128)(2,1)} async-done(((bf16[2048,704]{0,1:T(8,128)(2,1)}), bf16[512,704]{0,1:T(8,128)(2,1)}) %reduce-scatter.28.cloned.1.call-update) | async-done | bytes 720912 | tf_op jit(solution)/shard_map/reduce_scatter | solution.py:265
  657.0 63.6 %reduce-scatter.34.cloned.1.call-done = bf16[128,256]{1,0:T(8,128)(2,1)} async-done(((bf16[1024,256]{1,0:T(8,128)(2,1)}), bf16[128,256]{1,0:T(8,128)(2,1)}) %reduce-scatter.34.cloned.1.call-update) | async-done | bytes 65552
  723.1 27.3 %all_gather.27 = bf16[1024,256]{0,1:T(8,128)(2,1)S(1)} all-gather(bf16[128,256]{0,1:T(8,128)(2,1)S(1)} %pad_maximum_fusion.5), channel_id=1, replica_groups=mesh['dp'=4,'tensor'=8] {'tensor'}, dimensions={0}, use_global_device_ids=true | all-gather | bytes 589824 | tf_op jit(solution)/shard_map/all_gather | solution.py:228
  754.4 20.2 %reduce-scatter.22.cloned.1.call-done = bf16[512,256]{1,0:T(8,128)(2,1)} async-done(((bf16[2048,256]{1,0:T(8,128)(2,1)}), bf16[512,256]{1,0:T(8,128)(2,1)}) %reduce-scatter.22.cloned.1.call-update) | async-done | bytes 262160 | tf_op jit(solution)/shard_map/reduce_scatter | solution.py:259
  776.4 89.8 %reduce-scatter.20.cloned.1.call-done = bf16[128,2048]{1,0:T(8,128)(2,1)} async-done(((bf16[1024,2048]{1,0:T(8,128)(2,1)}), bf16[128,2048]{1,0:T(8,128)(2,1)}) %reduce-scatter.20.cloned.1.call-update) | async-done | bytes 524304 | tf_op jit(solution)/shard_map/reduce_scatter | solution.py:238
  869.1 73.9 %all-gather.1 = f32[32,2,2048]{2,1,0:T(2,128)S(1)} all-gather(f32[1,2,2048]{2,1,0:T(2,128)S(1)} %maximum_bitcast_fusion.1), channel_id=2, replica_groups=mesh['dp'=4,'tensor'=8] {'dp','tensor'}, dimensions={0}, use_global_device_ids=true | all-gather | bytes 540672 | tf_op jit(solution)/shard_map/all_gather | solution.py:256
  943.6 18.5 %reduce-scatter.16.cloned.1.call-done = bf16[128,2048]{1,0:T(8,128)(2,1)} async-done(((bf16[1024,2048]{1,0:T(8,128)(2,1)}), bf16[128,2048]{1,0:T(8,128)(2,1)}) %reduce-scatter.16.cloned.1.call-update) | async-done | bytes 524304 | tf_op jit(solution)/shard_map/reduce_scatter | solution.py:149
  962.2 3.8 fusion.57
  965.9 18.9 %reduce-scatter.24.cloned.1.call-done = f32[64,256]{1,0:T(8,128)} async-done(((f32[256,256]{1,0:T(8,128)}), f32[64,256]{1,0:T(8,128)}) %reduce-scatter.24.cloned.1.call-update) | async-done | bytes 65552 | tf_op jit(solution)/shard_map/reduce_scatter | solution.py:253
  (205 shorter events, 91.1 us)
Async XLA Ops:
  7.2 349.5 %copy-start = (bf16[704,2048]{1,0:T(8,128)(2,1)S(1)}, bf16[704,2048]{1,0:T(8,128)(2,1)}, u32[]{:S(2)}) copy-start(bf16[704,2048]{1,0:T(8,128)(2,1)} %param.21) | copy-start | bytes 8650756
  7.2 79.7 %all-gather.7.cloned.1.call-start = ((), (), s32[]{:S(2)}) async-start(), calls=%async_computation.11 | async-start | bytes 4718592 | tf_op jit(solution)/shard_map/all_gather | solution.py:61
  10.7 194.3 %reduce-scatter.14.cloned.1.call-start = ((), (), s32[]{:S(2)}) async-start(), calls=%async_computation.12 | async-start | bytes 4718592 | tf_op jit(solution)/shard_map/reduce_scatter | solution.py:134
  93.5 5.8 copy-start.20
  93.5 5.8 copy-start.21
  115.4 89.6 %copy-start.5 = (bf16[128,2048]{1,0:T(8,128)(2,1)S(1)}, bf16[128,2048]{1,0:T(8,128)(2,1)}, u32[]{:S(2)}) copy-start(bf16[128,2048]{1,0:T(8,128)(2,1)} %param.12) | copy-start | bytes 1572868
  118.7 88.1 %copy-start.26 = (f32[2048]{0:T(1024)S(1)}, f32[2048]{0:T(1024)}, u32[]{:S(2)}) copy-start(f32[2048]{0:T(1024)} %param.18) | copy-start | bytes 24580
  118.7 163.5 %all-gather.9.cloned.1.call-start = ((), (), s32[]{:S(2)}) async-start(), calls=%async_computation.13 | async-start | bytes 4718592 | tf_op jit(solution)/shard_map/all_gather | solution.py:61
  208.9 147.8 %all-gather.11.cloned.1.call-start = ((), (), s32[]{:S(2)}) async-start(), calls=%async_computation.15 | async-start | bytes 4718592 | tf_op jit(solution)/shard_map/all_gather | solution.py:65
  209.0 81.2 %copy-start.36 = (f32[128]{0:T(128)}, f32[128]{0:T(128)S(1)}, u32[]{:S(2)}) copy-start(f32[128]{0:T(128)S(1)} %dynamic_slice.16) | copy-start | bytes 1540
  211.1 249.6 %reduce-scatter.18.cloned.1.call-start = ((), (), s32[]{:S(2)}) async-start(), calls=%async_computation.16 | async-start | bytes 4718592 | tf_op jit(solution)/shard_map/reduce_scatter | solution.py:164
  282.2 8.0 copy-start.42
  282.2 8.0 copy-start.43
  356.7 8.5 copy-start.44
  374.1 86.5 %copy-start.34 = (f32[128]{0:T(128)S(1)}, f32[128]{0:T(128)}, u32[]{:S(2)}) copy-start(f32[128]{0:T(128)} %copy-done.33) | copy-start | bytes 1540
  374.1 165.3 %all-gather.13.cloned.1.call-start = ((), (), s32[]{:S(2)}) async-start(), calls=%async_computation.17 | async-start | bytes 4718592 | tf_op jit(solution)/shard_map/all_gather | solution.py:65
  466.1 128.7 %reduce-scatter.32.cloned.1.call-start = ((), (), s32[]{:S(2)}) async-start(), calls=%async_computation.24 | async-start | bytes 3604480 | tf_op jit(solution)/shard_map/reduce_scatter | solution.py:271
  473.5 142.1 %reduce-scatter.30.cloned.1.call-start = ((), (), s32[]{:S(2)}) async-start(), calls=%async_computation.23 | async-start | bytes 3604480 | tf_op jit(solution)/shard_map/reduce_scatter | solution.py:268
  490.7 163.9 %reduce-scatter.28.cloned.1.call-start = ((), (), s32[]{:S(2)}) async-start(), calls=%async_computation.22 | async-start | bytes 3604480 | tf_op jit(solution)/shard_map/reduce_scatter | solution.py:265
  498.1 222.5 %reduce-scatter.34.cloned.1.call-start = ((), (), s32[]{:S(2)}) async-start(), calls=%async_computation.25 | async-start | bytes 589824
  555.5 197.1 %reduce-scatter.26.cloned.1.call-start = ((), (), s32[]{:S(2)}) async-start(), calls=%async_computation.21 | async-start | bytes 1310720 | tf_op jit(solution)/shard_map/reduce_scatter | solution.py:262
  560.2 214.4 %reduce-scatter.22.cloned.1.call-start = ((), (), s32[]{:S(2)}) async-start(), calls=%async_computation.19 | async-start | bytes 1310720 | tf_op jit(solution)/shard_map/reduce_scatter | solution.py:259
  560.5 5.3 copy-start.12
  574.0 292.1 %reduce-scatter.20.cloned.1.call-start = ((), (), s32[]{:S(2)}) async-start(), calls=%async_computation.18 | async-start | bytes 4718592 | tf_op jit(solution)/shard_map/reduce_scatter | solution.py:238
  578.9 383.3 %reduce-scatter.16.cloned.1.call-start = ((), (), s32[]{:S(2)}) async-start(), calls=%async_computation.14 | async-start | bytes 4718592 | tf_op jit(solution)/shard_map/reduce_scatter | solution.py:149
  585.4 399.5 %reduce-scatter.24.cloned.1.call-start = ((), (), s32[]{:S(2)}) async-start(), calls=%async_computation.20 | async-start | bytes 327680 | tf_op jit(solution)/shard_map/reduce_scatter | solution.py:253
  597.2 269.0 %copy-start.27 = (f32[2048]{0:T(1024)S(1)}, f32[2048]{0:T(1024)}, u32[]{:S(2)}) copy-start(f32[2048]{0:T(1024)} %param.14) | copy-start | bytes 24580
  722.2 146.8 %copy-start.30 = (f32[2048]{0:T(1024)S(1)}, f32[2048]{0:T(1024)}, u32[]{:S(2)}) copy-start(f32[2048]{0:T(1024)} %get-tuple-element.12) | copy-start | bytes 24580
  722.2 239.9 %copy-start.35 = (f32[128]{0:T(128)S(1)}, f32[128]{0:T(128)}, u32[]{:S(2)}) copy-start(f32[128]{0:T(128)} %copy-done.33) | copy-start | bytes 1540
  722.2 239.9 %copy-start.37 = (f32[128]{0:T(128)S(1)}, f32[128]{0:T(128)}, u32[]{:S(2)}) copy-start(f32[128]{0:T(128)} %copy-done.36) | copy-start | bytes 1540
  722.2 239.9 %copy-start.39 = (f32[128]{0:T(128)S(1)}, f32[128]{0:T(128)}, u32[]{:S(2)}) copy-start(f32[128]{0:T(128)} %copy-done.38) | copy-start | bytes 1540
  722.3 239.9 %copy-start.41 = (f32[128]{0:T(128)S(1)}, f32[128]{0:T(128)}, u32[]{:S(2)}) copy-start(f32[128]{0:T(128)} %copy-done.40) | copy-start | bytes 1540
  (31 other events, 73.5 us)
Sparse Core Ops, SparseCore 0:
  10.8 76.0 all-gather.6
  118.8 86.1 reduce-scatter.13
  209.0 73.1 all-gather.8
  285.0 71.6 all-gather.10
  374.3 86.3 reduce-scatter.17
  466.2 73.1 all-gather.12
  541.9 34.6 reduce-scatter.31
  579.3 36.3 reduce-scatter.29
  618.2 36.3 reduce-scatter.27
  658.7 61.8 reduce-scatter.33
  723.1 23.9 reduce-scatter.25
  749.6 24.9 reduce-scatter.21
  778.2 87.8 reduce-scatter.19
  870.1 92.0 reduce-scatter.15
  965.0 19.7 reduce-scatter.23
